TPU v7x, 32 devices: a whole 2x2x4 slice. The times are simulated.
32 devices in a mesh: groups: 2 (over x), win: 4 (over y, core), rcv: 4 (over z).
Axes of the slice: x: 2, y: 2, z: 4, core: 2. Of those that a mesh axis runs over, the one named last changes fastest.
Arguments:
- traces: bfloat16 [32, 768, 4096], P('win', ('groups', 'rcv')), parts along dimension 1, may hold values from -6 to 6
- valid: int32 [64], P(('groups', 'win')), parts along dimension 0, may hold values 0 or 1
- src_station: int32 [64], P('groups'), parts along dimension 0, may hold values from 0 to 383, as said below
Outputs:
- stacks: float32 [32, 768, 2, 512], P(None, ('groups', 'rcv'), None, 'win'), parts along dimension 1
There are 2 independent parts, one for each index of `groups`. A program takes and returns all parts, laid end to end along the dimension named above; each array names one. Nothing has to cross between parts.
Inputs may be any that keep to these rules, and one draw needn't show every extreme that they name: `src_station`: distinct stations; station 0 and station 384 - 1 are always among them.
All inputs are finite; a program needn't handle non-finite values. No bound on the sum of `valid` on one device may be relied on, other than what follows from the above.
Results may differ from a plain program's by a relative error of at most 0.0049.
Values may be sent and summed in bfloat16 or wider, within the bound.
No kernel may reach another device: no remote copies, remote signals or barrier semaphores. Data moves between devices by JAX's collectives and lax.ppermute only.
A program may use at most 128 MiB of HBM per device.

v0:
```python
import math

import jax
import jax.numpy as jnp
from jax import lax
from jax.sharding import PartitionSpec as P

F = 512


def band_table(count, bins, first):
    samples = jnp.arange(count, dtype=jnp.int32)
    freqs = first + jnp.arange(bins, dtype=jnp.int32)
    phase = samples[:, None] * freqs[None, :] % count
    angle = phase.astype(jnp.float32) * (2.0 * math.pi / count)
    return jnp.concatenate([jnp.cos(angle), -jnp.sin(angle)], axis=1).astype(jnp.bfloat16)


def correlate(received, sources):
    rr = received[:, :, 0]
    ri = received[:, :, 1]
    sr = sources[:, :, 0]
    si = sources[:, :, 1]
    real = jnp.einsum("wsf,wrf->srf", sr, rr, preferred_element_type=jnp.float32)
    real = real + jnp.einsum("wsf,wrf->srf", si, ri, preferred_element_type=jnp.float32)
    imag = jnp.einsum("wsf,wrf->srf", sr, ri, preferred_element_type=jnp.float32)
    imag = imag - jnp.einsum("wsf,wrf->srf", si, rr, preferred_element_type=jnp.float32)
    return jnp.stack([real, imag], axis=2)


def body(traces, valid, src_station):
    w_dev, r_dev, samples = traces.shape
    bins = F
    table = band_table(samples, bins, samples // 16)
    spectra = jnp.dot(
        traces.reshape(w_dev * r_dev, samples), table, preferred_element_type=jnp.float32
    )
    spectra = spectra.reshape(w_dev, r_dev, 2, bins)
    power = jnp.sum(spectra * spectra, axis=(2, 3), keepdims=True) / bins
    white = (spectra * lax.rsqrt(power + 1e-06)).astype(jnp.bfloat16)
    received = white * valid.astype(jnp.bfloat16)[:, None, None, None]
    offset = lax.axis_index("rcv") * r_dev
    station_ids = offset + jnp.arange(r_dev, dtype=jnp.int32)
    selector = (src_station[:, None] == station_ids[None, :]).astype(jnp.bfloat16)
    local_rows = jnp.einsum("sr,wrcf->wscf", selector, white, preferred_element_type=jnp.float32)
    sources = lax.psum(local_rows.astype(jnp.bfloat16), "rcv")
    scale = 1.0 / math.sqrt(w_dev * lax.axis_size("win"))
    partial_stacks = correlate(received, sources)
    stacks = lax.psum_scatter(partial_stacks, "win", scatter_dimension=3, tiled=True)
    return stacks * scale


def solution(mesh):
    return jax.shard_map(
        body,
        mesh=mesh,
        in_specs=(P("win", ("groups", "rcv"), None), P(("groups", "win")), P("groups")),
        out_specs=P(None, ("groups", "rcv"), None, "win"),
        check_vma=False,
    )
```

profile of v0, /device:TPU:0, one launch (start us, length us, event | category | flops | bytes accessed | tf_op | source)
XLA Modules:
  0.0 262.6 jit_solution(9068600715958366044)
XLA Ops:
  6.5 0.7 convert_element_type.21
  7.2 34.0 %cosine_convert_fusion = (bf16[4096,512]{1,0:T(8,128)(2,1)S(1)}, bf16[4096,512]{1,0:T(8,128)(2,1)S(1)}) fusion(s32[512]{0:T(512)S(1)} %iota_add_fusion), kind=kLoop, calls=%fused_computation.15 | loop fusion | flops 35651584 | bytes 8390656 | tf_op jit(solution)/shard_map/convert
  41.2 9.5 %multiply_reduce_fusion = (f32[768]{0:T(1024)S(1)}, f32[768,1024]{0,1:T(8,128)S(1)}) fusion(bf16[768,4096]{1,0:T(8,128)(2,1)} %bitcast.45, bf16[4096,512]{1,0:T(8,128)(2,1)S(1)} %get-tuple-element.10, bf16[4096,512]{1,0:T(8,128)(2,1)S(1)} %get-tuple-element.9), kind=kOutput, calls=%fused_computation.20 | convolution fusion | flops 6460800000 | bytes 17828864 | tf_op jit(solution)/shard_map/dot_general | solution.py:35
  50.7 0.1 rsqrt.12
  50.8 3.1 %reshape.36 = f32[8,96,2,512]{1,0,3,2:T(8,128)} reshape(f32[768,1024]{0,1:T(8,128)S(1)} %get-tuple-element.12) | data formatting | bytes 6291456 | tf_op jit(solution)/shard_map/reshape | solution.py:38
  53.9 2.9 %broadcast_multiply_fusion.1 = (bf16[8,96,2,512]{1,0,3,2:T(8,128)(2,1)S(1)}, bf16[8,96,2,512]{1,0,3,2:T(8,128)(2,1)S(1)}) fusion(bf16[8]{0:T(256)(128)(2,1)S(1)} %convert_element_type.21, f32[8,96,2,512]{1,0,3,2:T(8,128)} %reshape.36, f32[8,96]{1,0:T(8,128)S(1)} %rsqrt.12), kind=kLoop, calls=%fused_computation.29 | loop fusion | flops 2359296 | bytes 6294544 | tf_op jit(solution)/shard_map/mul | solution.py:41
  56.8 1.6 fusion.18
  58.5 0.2 reduce-scatter.4.cloned.1.call-start
  58.7 40.9 %all-reduce.2.cloned.1.call-done = bf16[8,32,2,512]{3,1,2,0:T(8,128)(2,1)} async-done(((bf16[8,32,2,512]{3,1,2,0:T(8,128)(2,1)}), bf16[8,32,2,512]{3,1,2,0:T(8,128)(2,1)}) %all-reduce.2.cloned.1.call-update) | async-done | bytes 524304 | tf_op jit(solution)/shard_map/psum | solution.py:46
  99.7 1.8 slice_bitcast_fusion.6
  101.4 1.7 copy.29
  103.2 4.0 %fusion.22 = f32[512,96,32]{1,2,0:T(8,128)} fusion(bf16[8,32,512]{1,0,2:T(8,128)(2,1)S(1)} %copy.29, bf16[8,96,2,512]{1,0,3,2:T(8,128)(2,1)S(1)} %get-tuple-element.5), kind=kOutput, calls=%fused_computation.31 | convolution fusion | flops 25165824 | bytes 8388608 | tf_op jit(solution)/shard_map/wsf,wrf->srf/dot_general | solution.py:26
  107.2 4.0 %fusion.21 = f32[512,96,32]{1,2,0:T(8,128)} fusion(bf16[8,32,512]{1,0,2:T(8,128)(2,1)S(1)} %copy.29, bf16[8,96,2,512]{1,0,3,2:T(8,128)(2,1)S(1)} %get-tuple-element.5), kind=kOutput, calls=%fused_computation.30 | convolution fusion | flops 25165824 | bytes 8388608 | tf_op jit(solution)/shard_map/wsf,wrf->srf/dot_general | solution.py:24
  111.2 0.8 copy.30
  111.9 4.4 %subtract_bitcast_fusion = f32[32,96,1,512]{1,0,3,2:T(8,128)S(1)} fusion(f32[512,96,32]{1,2,0:T(8,128)} %fusion.22, bf16[8,32,512]{1,0,2:T(8,128)(2,1)S(1)} %copy.30, bf16[8,96,2,512]{1,0,3,2:T(8,128)(2,1)S(1)} %get-tuple-element.5), kind=kOutput, calls=%fused_computation.12 | convolution fusion | flops 26738688 | bytes 14680064 | tf_op jit(solution)/shard_map/wsf,wrf->srf/dot_general | solution.py:27
  116.3 1.4 copy-done
  117.8 1.3 add_bitcast_fusion
  119.1 6.3 %copy_bitcast_fusion = f32[512,2,32,96]{3,2,1,0:T(8,128)} fusion(f32[32,96,1,512]{1,0,3,2:T(8,128)S(1)} %subtract_bitcast_fusion, f32[32,96,1,512]{1,0,3,2:T(8,128)S(1)} %add_bitcast_fusion), kind=kLoop, calls=%fused_computation.1 | loop fusion | flops 3145728 | bytes 25165824
  125.4 17.7 %reshape.37 = f32[512,6144]{1,0:T(8,128)} reshape(f32[512,2,32,96]{3,2,1,0:T(8,128)} %copy_bitcast_fusion) | data formatting | bytes 25165824
  143.1 99.2 %reduce-scatter.4.cloned.1.call-done = f32[128,6144]{1,0:T(8,128)} async-done(((f32[512,6144]{1,0:T(8,128)}), f32[128,6144]{1,0:T(8,128)}) %reduce-scatter.4.cloned.1.call-update) | async-done | bytes 3145744
  242.3 5.4 %reshape.38 = f32[128,2,32,96]{3,2,1,0:T(8,128)} reshape(f32[128,6144]{1,0:T(8,128)} %reduce-scatter.4.cloned.1.call-done) | data formatting | bytes 6291456
  247.6 3.7 %copy.33 = f32[32,96,2,128]{3,1,2,0:T(8,128)S(1)} copy(f32[32,96,2,128]{1,0,2,3:T(8,128)} %bitcast.44) | data formatting | bytes 6291456 | tf_op jit(solution)/shard_map/reduce_scatter | solution.py:49
  251.4 0.3 broadcast_multiply_fusion
  251.7 4.1 %copy.34 = f32[32,96,2,128]{3,2,1,0:T(2,128)} copy(f32[32,96,2,128]{3,1,2,0:T(8,128)S(1)} %broadcast_multiply_fusion) | data formatting | bytes 6291456 | tf_op jit(solution)/shard_map/mul | solution.py:50
  (9 shorter events, 0.1 us)
Async XLA Ops:
  6.5 93.1 %all-reduce.2.cloned.1.call-start = ((), (), s32[]{:S(2)}) async-start(), calls=%async_computation.1 | async-start | bytes 1048576 | tf_op jit(solution)/shard_map/psum | solution.py:46
  50.7 6.1 %copy-start.1 = (s32[32]{0:T(128)S(1)}, s32[32]{0:T(128)}, u32[]{:S(2)}) copy-start(s32[32]{0:T(128)} %param.5) | copy-start | bytes 388
  58.5 183.8 %reduce-scatter.4.cloned.1.call-start = ((), (), s32[]{:S(2)}) async-start(), calls=%async_computation.2 | async-start | bytes 15728640
  111.9 5.8 %copy-start = (f32[512,96,32]{1,2,0:T(8,128)S(1)}, f32[512,96,32]{1,2,0:T(8,128)}, u32[]{:S(2)}) copy-start(f32[512,96,32]{1,2,0:T(8,128)} %fusion.21) | copy-start | bytes 18874372
Sparse Core Ops, SparseCore 0:
  58.6 40.9 all-reduce.1
  143.2 99.0 reduce-scatter.3
where the time goes:
time: 263 us
  waiting for transfers between devices  140 us (53%)
  other arithmetic  44.1 us (17%)
  local copies, waits for them, and re-layouts  39.8 us (15%)
  matrix products  24.8 us (9%)
  between operations  13.5 us (5%)
    unnamed x3, waiting for transfers between devices  99.2 us
    psum x1, waiting for transfers between devices, body(): sources = lax.psum(local_rows.astype(jnp.bfloat16), 'rcv')  40.9 us
    another operation x1, other arithmetic  34 us
    unnamed x6, local copies, waits for them, and re-layouts  24.5 us
    dot_general x1, matrix products, body(): jnp.dot(traces.reshape(w_dev * r_dev, samples), table, preferred_element_...  9.49 us
    unnamed x1, other arithmetic  6.25 us
  transfers between devices with their start and end apart: 2, of which 2 were waited for; matrix products, arithmetic and copies ran while one was open for 0% of the time, Pallas kernels for 0%

commit v1 on v0

v1 whole, which is shorter than its diff:
```python
import math

import jax
import jax.numpy as jnp
import numpy as np
from jax import lax
from jax.sharding import PartitionSpec as P

F = 512


def band_table(count, bins, first):
    samples = np.arange(count, dtype=np.int64)
    freqs = first + np.arange(bins, dtype=np.int64)
    phase = samples[:, None] * freqs[None, :] % count
    angle = phase.astype(np.float64) * (2.0 * math.pi / count)
    return np.concatenate([np.cos(angle), -np.sin(angle)], axis=1).astype(jnp.bfloat16)


def correlate(received, sources):
    rr = received[:, :, 0]
    ri = received[:, :, 1]
    sr = sources[:, :, 0]
    si = sources[:, :, 1]
    real = jnp.einsum("wsf,wrf->srf", sr, rr, preferred_element_type=jnp.float32)
    real = real + jnp.einsum("wsf,wrf->srf", si, ri, preferred_element_type=jnp.float32)
    imag = jnp.einsum("wsf,wrf->srf", sr, ri, preferred_element_type=jnp.float32)
    imag = imag - jnp.einsum("wsf,wrf->srf", si, rr, preferred_element_type=jnp.float32)
    return jnp.stack([real, imag], axis=2)


def body(traces, valid, src_station):
    w_dev, r_dev, samples = traces.shape
    bins = F
    n_win = lax.axis_size("win")
    n_rcv = lax.axis_size("rcv")
    bins_dev = bins // n_win
    table = jnp.asarray(band_table(samples, bins, samples // 16))
    spectra = jnp.dot(
        traces.reshape(w_dev * r_dev, samples), table, preferred_element_type=jnp.float32
    )
    spectra = spectra.reshape(w_dev, r_dev, 2, bins)
    power = jnp.sum(spectra * spectra, axis=(2, 3), keepdims=True) / bins
    gain = lax.rsqrt(power + 1e-06)
    keep = valid.astype(jnp.float32)[:, None, None, None]
    white = ((spectra * gain) * keep).astype(jnp.bfloat16)
    blocks = white.reshape(w_dev, r_dev, 2, n_win, bins_dev).transpose(3, 0, 1, 2, 4)

    me = lax.axis_index("win")
    parts = []
    for j in range(n_win):
        block = lax.dynamic_index_in_dim(blocks, me ^ j, 0, keepdims=False)
        if j:
            block = lax.ppermute(block, "win", [(i, i ^ j) for i in range(n_win)])
        parts.append(block)

    offset = lax.axis_index("rcv") * r_dev
    station_ids = offset + jnp.arange(r_dev, dtype=jnp.int32)
    selector = (src_station[:, None] == station_ids[None, :]).astype(jnp.bfloat16)
    sources = []
    for part in parts:
        rows = jnp.einsum("sr,wrcf->wscf", selector, part, preferred_element_type=jnp.float32)
        rows = rows.astype(jnp.bfloat16)
        rows = lax.all_to_all(rows, "rcv", 0, 0, tiled=True)
        rows = rows.reshape((n_rcv, w_dev // n_rcv) + rows.shape[1:])
        merged = jnp.sum(rows.astype(jnp.float32), axis=0).astype(jnp.bfloat16)
        sources.append(lax.all_gather(merged, "rcv", axis=0, tiled=True))
    scale = 1.0 / math.sqrt(w_dev * n_win)
    stacks = correlate(jnp.concatenate(parts, axis=0), jnp.concatenate(sources, axis=0))
    return stacks * scale


def solution(mesh):
    return jax.shard_map(
        body,
        mesh=mesh,
        in_specs=(P("win", ("groups", "rcv"), None), P(("groups", "win")), P("groups")),
        out_specs=P(None, ("groups", "rcv"), None, "win"),
        check_vma=False,
    )
```

time: 263 us -> 147 us (0.56)
  waiting for transfers between devices: 140 us -> 12.7 us
  blocking collectives: 0 us -> 54.6 us
  other arithmetic: 44.1 us -> 6.02 us
  starting transfers between devices: 0.22 us -> 18 us
  between operations: 13.5 us -> 0.21 us
  local copies, waits for them, and re-layouts: 39.8 us -> 32.2 us
    unnamed x3 -> x0, waiting for transfers between devices: 99.2 us -> none
    all_gather x0 -> x4, blocking collectives: none -> 54.6 us  [body(): sources.append(lax.all_gather(merged, 'rcv', axis=0, tiled=True))]
    psum x1 -> x0, waiting for transfers between devices: 40.9 us -> none  [body(): sources = lax.psum(local_rows.astype(jnp.bfloat16), 'rcv')]
    another operation x1, other arithmetic: 34 us -> 3.41 us  [correlate(): return jnp.stack([real, imag], axis=2)]
    unnamed x6 -> x15, local copies, waits for them, and re-layouts: 24.5 us -> 6.18 us
    all_to_all x0 -> x4, starting transfers between devices: none -> 15.9 us  [body(): rows = lax.all_to_all(rows, 'rcv', 0, 0, tiled=True)]
    all_to_all x0 -> x4, waiting for transfers between devices: none -> 12.7 us  [body(): rows = lax.all_to_all(rows, 'rcv', 0, 0, tiled=True)]
    dot_general x0 -> x4, local copies, waits for them, and re-layouts: none -> 9.79 us  [the longest x1 3.07 us: correlate(): jnp.einsum('wsf,wrf->srf', sr, rr, preferred_element_type=jnp.float32)]
  transfers between devices with their start and end apart: 2 -> 7, of which waited for: 2 -> 3; matrix products, arithmetic and copies ran while one was open for 0% -> 8% of each run, Pallas kernels for 0% -> 0%
where the time goes in v1:
time: 147 us
  blocking collectives  54.6 us (37%)
  local copies, waits for them, and re-layouts  32.2 us (22%)
  matrix products  23 us (16%)
  starting transfers between devices  18 us (12%)
  waiting for transfers between devices  12.7 us (9%)
  other arithmetic  6.02 us (4%)
    all_gather x4, blocking collectives, body(): sources.append(lax.all_gather(merged, 'rcv', axis=0, tiled=True))  54.6 us
    all_to_all x4, starting transfers between devices, body(): rows = lax.all_to_all(rows, 'rcv', 0, 0, tiled=True)  15.9 us
    all_to_all x4, waiting for transfers between devices, body(): rows = lax.all_to_all(rows, 'rcv', 0, 0, tiled=True)  12.7 us
    dot_general x1, matrix products, body(): jnp.dot(traces.reshape(w_dev * r_dev, samples), table, preferred_element_...  11.2 us
    unnamed x15, local copies, waits for them, and re-layouts  6.18 us
    another operation x5, local copies, waits for them, and re-layouts  6.16 us
    mul x1, local copies, waits for them, and re-layouts, body(): return stacks * scale  4.1 us
    dot_general x4, matrix products, body(): jnp.einsum('sr,wrcf->wscf', selector, part, preferred_element_type=jnp.fl...  3.57 us
  transfers between devices with their start and end apart: 7, of which 3 were waited for; matrix products, arithmetic and copies ran while one was open for 8% of the time, Pallas kernels for 0%

profile of v1, /device:TPU:0, one launch (start us, length us, event | category | flops | bytes accessed | tf_op | source)
XLA Modules:
  0.0 146.7 jit_solution(15009874956117573572)
XLA Ops:
  0.7 11.2 %multiply_reduce_fusion = (f32[8,96]{1,0:T(8,128)S(1)}, f32[2,512,8,96]{1,3,2,0:T(8,128)S(1)}) fusion(bf16[2,512,4096,1]{2,1,3,0:T(8,128)(2,1)} %constant.46, bf16[8,96,4096]{2,1,0:T(8,128)(2,1)} %param.4), kind=kOutput, calls=%fused_computation.4 | convolution fusion | flops 6444022784 | bytes 17828864 | tf_op jit(solution)/shard_map/dot_general | solution.py:39
  12.7 4.1 %constant_dynamic-slice_fusion.3 = (bf16[8,96,2,1,128]{4,3,1,0,2:T(2,128)(2,1)}, bf16[8,96,2,1,128]{4,3,1,0,2:T(2,128)(2,1)S(1)}, bf16[8,96,2,1,128]{4,3,1,0,2:T(2,128)(2,1)S(1)}, bf16[8,96,2,1,128]{4,3,1,0,2:T(2,128)(2,1)S(1)}) fusion(bf16[8,96,2,4,128]{4,3,1,0,2:T(4,128)(2,1)S(1)} %reshape.42, s32[]{:T(128)S(6)} %select_n.13, s32[]{:T(128)S(6)} %select_n.16, ...), kind=kLoop, calls=%fused_computation.55 | loop fusion | bytes 3145744 | tf_op jit(solution)/shard_map/dynamic-slice
  19.4 5.9 %all-to-all-start = ((bf16[8,32,2,128]{3,1,2,0:T(8,128)(2,1)}), bf16[8,32,2,128]{3,1,2,0:T(8,128)(2,1)S(1)}, u32[]{:S(2)}, u32[]{:S(2)}) async-start(bf16[8,32,2,128]{3,1,2,0:T(8,128)(2,1)} %fusion.3), calls=%async_computation | async-start | bytes 262144 | tf_op jit(solution)/shard_map/all_to_all | solution.py:64
  27.7 4.0 %all-to-all-done = bf16[8,32,2,128]{3,1,2,0:T(8,128)(2,1)S(1)} async-done(((bf16[8,32,2,128]{3,1,2,0:T(8,128)(2,1)}), bf16[8,32,2,128]{3,1,2,0:T(8,128)(2,1)S(1)}, u32[]{:S(2)}, u32[]{:S(2)}) %all-to-all-start) | async-done | bytes 131104 | tf_op jit(solution)/shard_map/all_to_all | solution.py:64
  31.7 13.5 %all_gather.12 = bf16[8,32,2,128]{3,1,2,0:T(8,128)(2,1)S(1)} all-gather(bf16[2,32,2,128]{3,1,2,0:T(8,128)(2,1)S(1)} %reduce_sum.58), channel_id=1, replica_groups=mesh['groups'=2,'win'=4,'rcv'=4] {'rcv'}, dimensions={0}, use_global_device_ids=true | all-gather | bytes 163840 | tf_op jit(solution)/shard_map/all_gather | solution.py:67
  46.8 3.3 %all-to-all-start.1 = ((bf16[8,32,2,128]{3,1,2,0:T(8,128)(2,1)}), bf16[8,32,2,128]{3,1,2,0:T(8,128)(2,1)S(1)}, u32[]{:S(2)}, u32[]{:S(2)}) async-start(bf16[8,32,2,128]{3,1,2,0:T(8,128)(2,1)} %fusion.4), calls=%async_computation.1 | async-start | bytes 262144 | tf_op jit(solution)/shard_map/all_to_all | solution.py:64
  52.3 3.8 %all-to-all-done.1 = bf16[8,32,2,128]{3,1,2,0:T(8,128)(2,1)S(1)} async-done(((bf16[8,32,2,128]{3,1,2,0:T(8,128)(2,1)}), bf16[8,32,2,128]{3,1,2,0:T(8,128)(2,1)S(1)}, u32[]{:S(2)}, u32[]{:S(2)}) %all-to-all-start.1) | async-done | bytes 131104 | tf_op jit(solution)/shard_map/all_to_all | solution.py:64
  56.0 3.3 %all-to-all-start.2 = ((bf16[8,32,2,128]{3,1,2,0:T(8,128)(2,1)}), bf16[8,32,2,128]{3,1,2,0:T(8,128)(2,1)S(1)}, u32[]{:S(2)}, u32[]{:S(2)}) async-start(bf16[8,32,2,128]{3,1,2,0:T(8,128)(2,1)} %fusion.5), calls=%async_computation.2 | async-start | bytes 262144 | tf_op jit(solution)/shard_map/all_to_all | solution.py:64
  60.3 5.0 %all-to-all-done.2 = bf16[8,32,2,128]{3,1,2,0:T(8,128)(2,1)S(1)} async-done(((bf16[8,32,2,128]{3,1,2,0:T(8,128)(2,1)}), bf16[8,32,2,128]{3,1,2,0:T(8,128)(2,1)S(1)}, u32[]{:S(2)}, u32[]{:S(2)}) %all-to-all-start.2) | async-done | bytes 131104 | tf_op jit(solution)/shard_map/all_to_all | solution.py:64
  65.2 3.3 %all-to-all-start.3 = ((bf16[8,32,2,128]{3,1,2,0:T(8,128)(2,1)}), bf16[8,32,2,128]{3,1,2,0:T(8,128)(2,1)S(1)}, u32[]{:S(2)}, u32[]{:S(2)}) async-start(bf16[8,32,2,128]{3,1,2,0:T(8,128)(2,1)} %fusion.6), calls=%async_computation.3 | async-start | bytes 262144 | tf_op jit(solution)/shard_map/all_to_all | solution.py:64
  69.6 1.9 %copy.30 = bf16[32,96,128]{1,0,2:T(8,128)(2,1)S(1)} copy(bf16[32,96,128]{2,1,0:T(8,128)(2,1)} %get-tuple-element.5) | data formatting | bytes 1572864 | tf_op jit(solution)/shard_map/squeeze | solution.py:21
  72.5 13.9 %all_gather.13 = bf16[8,32,2,128]{3,1,2,0:T(8,128)(2,1)S(1)} all-gather(bf16[2,32,2,128]{3,1,2,0:T(8,128)(2,1)S(1)} %reduce_sum.59), channel_id=1, replica_groups=mesh['groups'=2,'win'=4,'rcv'=4] {'rcv'}, dimensions={0}, use_global_device_ids=true | all-gather | bytes 163840 | tf_op jit(solution)/shard_map/all_gather | solution.py:67
  86.4 13.5 %all_gather.14 = bf16[8,32,2,128]{3,1,2,0:T(8,128)(2,1)S(1)} all-gather(bf16[2,32,2,128]{3,1,2,0:T(8,128)(2,1)S(1)} %reduce_sum.60), channel_id=1, replica_groups=mesh['groups'=2,'win'=4,'rcv'=4] {'rcv'}, dimensions={0}, use_global_device_ids=true | all-gather | bytes 163840 | tf_op jit(solution)/shard_map/all_gather | solution.py:67
  99.9 13.6 %all_gather.15 = bf16[8,32,2,128]{3,1,2,0:T(8,128)(2,1)S(1)} all-gather(bf16[2,32,2,128]{3,1,2,0:T(8,128)(2,1)S(1)} %reduce_sum.61), channel_id=1, replica_groups=mesh['groups'=2,'win'=4,'rcv'=4] {'rcv'}, dimensions={0}, use_global_device_ids=true | all-gather | bytes 163840 | tf_op jit(solution)/shard_map/all_gather | solution.py:67
  116.6 2.6 %copy.43 = bf16[32,32,1,128]{0,1,3,2:T(8,128)(2,1)} copy(bf16[32,32,1,128]{3,1,2,0:T(8,128)(2,1)S(1)} %get-tuple-element.11) | data formatting | bytes 524288
  120.8 3.0 %fusion.7 = f32[128,96,32]{1,2,0:T(8,128)} fusion(bf16[32,96,128]{1,0,2:T(8,128)(2,1)S(1)} %copy.32, bf16[32,32,1,128]{0,1,3,2:T(8,128)(2,1)} %copy.43), kind=kOutput, calls=%fused_computation.17 | convolution fusion | flops 25165824 | bytes 2621440 | tf_op jit(solution)/shard_map/wsf,wrf->srf/dot_general | solution.py:26
  123.9 1.7 %fusion.9 = f32[128,96,32]{1,2,0:T(8,128)} fusion(bf16[32,96,128]{1,0,2:T(8,128)(2,1)S(1)} %copy.30, bf16[32,32,1,128]{0,1,3,2:T(8,128)(2,1)S(1)} %copy-done), kind=kOutput, calls=%fused_computation.19 | convolution fusion | flops 25165824 | bytes 2621440 | tf_op jit(solution)/shard_map/wsf,wrf->srf/dot_general | solution.py:28
  125.6 1.8 %fusion.11 = f32[128,96,32]{1,2,0:T(8,128)} fusion(bf16[32,96,128]{1,0,2:T(8,128)(2,1)S(1)} %copy.30, bf16[32,32,1,128]{0,1,3,2:T(8,128)(2,1)S(1)} %copy.42), kind=kOutput, calls=%fused_computation.21 | convolution fusion | flops 25165824 | bytes 2621440 | tf_op jit(solution)/shard_map/wsf,wrf->srf/dot_general | solution.py:25
  129.1 3.1 %copy.34 = f32[128,96,32]{0,1,2:T(8,128)} copy(f32[128,96,32]{1,2,0:T(8,128)} %fusion.7) | data formatting | bytes 3145728 | tf_op jit(solution)/shard_map/wsf,wrf->srf/dot_general | solution.py:26
  132.2 1.8 %copy.38 = f32[128,96,32]{0,1,2:T(8,128)} copy(f32[128,96,32]{1,2,0:T(8,128)S(1)} %copy-done.1) | data formatting | bytes 3145728 | tf_op jit(solution)/shard_map/wsf,wrf->srf/dot_general | solution.py:28
  134.0 3.1 %copy.33 = f32[128,96,32]{0,1,2:T(8,128)} copy(f32[128,96,32]{1,2,0:T(8,128)} %fusion.11) | data formatting | bytes 3145728 | tf_op jit(solution)/shard_map/wsf,wrf->srf/dot_general | solution.py:25
  137.1 1.8 %copy.37 = f32[128,96,32]{0,1,2:T(8,128)} copy(f32[128,96,32]{1,2,0:T(8,128)S(1)} %copy-done.2) | data formatting | bytes 3145728 | tf_op jit(solution)/shard_map/wsf,wrf->srf/dot_general | solution.py:27
  138.9 3.4 %subtract_bitcast_fusion = (f32[32,96,1,128]{3,1,2,0:T(8,128)S(1)}, f32[32,96,1,128]{3,1,2,0:T(8,128)S(1)}) fusion(f32[128,96,32]{0,1,2:T(8,128)} %copy.37, f32[128,96,32]{0,1,2:T(8,128)} %copy.38, f32[128,96,32]{0,1,2:T(8,128)} %copy.33, f32[128,96,32]{0,1,2:T(8,128)} %copy.34), kind=kLoop, calls=%fused_computation.7 | loop fusion | flops 786432 | bytes 9437184 | tf_op jit(solution)/shard_map/stack | solution.py:29
  142.6 4.1 %copy.39 = f32[32,96,2,128]{3,2,1,0:T(2,128)} copy(f32[32,96,2,128]{3,1,2,0:T(8,128)S(1)} %maximum_multiply_fusion) | data formatting | bytes 6291456 | tf_op jit(solution)/shard_map/mul | solution.py:70
  (45 shorter events, 19.9 us)
Async XLA Ops:
  16.7 1.8 %copy-start.4 = (s32[32]{0:T(128)S(1)}, s32[32]{0:T(128)}, u32[]{:S(2)}) copy-start(s32[32]{0:T(128)} %param.6) | copy-start | bytes 388
  16.8 29.1 %collective-permute-start = (bf16[8,96,2,128]{3,1,2,0:T(8,128)(2,1)S(1)}, bf16[8,96,2,128]{3,1,2,0:T(8,128)(2,1)S(1)}, u32[]{:S(2)}, u32[]{:S(2)}) collective-permute-start(bf16[8,96,2,128]{3,1,2,0:T(8,128)(2,1)S(1)} %bitcast.86), channel_id=1, source_target_pairs={{0,4},{4,0},{8,12},{12,8},{1,5},{5,1},{9,13},{13,9},{2,6},{6,2},{1... | collective-permute-start | bytes 1179656 | tf_op jit(solution)/shard_map/ppermute | solution.py:54
  19.4 12.3 %all-to-all-start = ((bf16[8,32,2,128]{3,1,2,0:T(8,128)(2,1)}), bf16[8,32,2,128]{3,1,2,0:T(8,128)(2,1)S(1)}, u32[]{:S(2)}, u32[]{:S(2)}) async-start(bf16[8,32,2,128]{3,1,2,0:T(8,128)(2,1)} %fusion.3), calls=%async_computation | async-start | bytes 262144 | tf_op jit(solution)/shard_map/all_to_all | solution.py:64
  25.3 24.8 %collective-permute-start.1 = (bf16[8,96,2,128]{3,1,2,0:T(8,128)(2,1)S(1)}, bf16[8,96,2,128]{3,1,2,0:T(8,128)(2,1)S(1)}, u32[]{:S(2)}, u32[]{:S(2)}) collective-permute-start(bf16[8,96,2,128]{3,1,2,0:T(8,128)(2,1)S(1)} %bitcast.87), channel_id=1, source_target_pairs={{0,8},{4,12},{8,0},{12,4},{1,9},{5,13},{9,1},{13,5},{2,10},{6,14},... | collective-permute-start | bytes 1179656 | tf_op jit(solution)/shard_map/ppermute | solution.py:54
  27.7 22.4 %collective-permute-start.2 = (bf16[8,96,2,128]{3,1,2,0:T(8,128)(2,1)}, bf16[8,96,2,128]{3,1,2,0:T(8,128)(2,1)S(1)}, u32[]{:S(2)}, u32[]{:S(2)}) collective-permute-start(bf16[8,96,2,128]{3,1,2,0:T(8,128)(2,1)} %bitcast.76), channel_id=1, source_target_pairs={{0,12},{4,8},{8,4},{12,0},{1,13},{5,9},{9,5},{13,1},{2,14},{6,10},... | collective-permute-start | bytes 1179656 | tf_op jit(solution)/shard_map/ppermute | solution.py:54
  45.9 4.2 %copy-start.3 = (bf16[8,96,2,128]{3,1,2,0:T(8,128)(2,1)}, bf16[8,96,2,128]{3,1,2,0:T(8,128)(2,1)S(1)}, u32[]{:S(2)}) copy-start(bf16[8,96,2,128]{3,1,2,0:T(8,128)(2,1)S(1)} %collective-permute-done) | copy-start | bytes 1179652
  46.8 9.2 %all-to-all-start.1 = ((bf16[8,32,2,128]{3,1,2,0:T(8,128)(2,1)}), bf16[8,32,2,128]{3,1,2,0:T(8,128)(2,1)S(1)}, u32[]{:S(2)}, u32[]{:S(2)}) async-start(bf16[8,32,2,128]{3,1,2,0:T(8,128)(2,1)} %fusion.4), calls=%async_computation.1 | async-start | bytes 262144 | tf_op jit(solution)/shard_map/all_to_all | solution.py:64
  56.0 9.2 %all-to-all-start.2 = ((bf16[8,32,2,128]{3,1,2,0:T(8,128)(2,1)}), bf16[8,32,2,128]{3,1,2,0:T(8,128)(2,1)S(1)}, u32[]{:S(2)}, u32[]{:S(2)}) async-start(bf16[8,32,2,128]{3,1,2,0:T(8,128)(2,1)} %fusion.5), calls=%async_computation.2 | async-start | bytes 262144 | tf_op jit(solution)/shard_map/all_to_all | solution.py:64
  65.2 34.6 %all-to-all-start.3 = ((bf16[8,32,2,128]{3,1,2,0:T(8,128)(2,1)}), bf16[8,32,2,128]{3,1,2,0:T(8,128)(2,1)S(1)}, u32[]{:S(2)}, u32[]{:S(2)}) async-start(bf16[8,32,2,128]{3,1,2,0:T(8,128)(2,1)} %fusion.6), calls=%async_computation.3 | async-start | bytes 262144 | tf_op jit(solution)/shard_map/all_to_all | solution.py:64
  120.8 3.1 %copy-start = (bf16[32,32,1,128]{0,1,3,2:T(8,128)(2,1)S(1)}, bf16[32,32,1,128]{0,1,3,2:T(8,128)(2,1)}, u32[]{:S(2)}) copy-start(bf16[32,32,1,128]{0,1,3,2:T(8,128)(2,1)} %copy.43) | copy-start | bytes 786436
  129.1 3.1 %copy-start.1 = (f32[128,96,32]{1,2,0:T(8,128)S(1)}, f32[128,96,32]{1,2,0:T(8,128)}, u32[]{:S(2)}) copy-start(f32[128,96,32]{1,2,0:T(8,128)} %fusion.9) | copy-start | bytes 4718596
  134.0 3.1 %copy-start.2 = (f32[128,96,32]{1,2,0:T(8,128)S(1)}, f32[128,96,32]{1,2,0:T(8,128)}, u32[]{:S(2)}) copy-start(f32[128,96,32]{1,2,0:T(8,128)} %fusion.13) | copy-start | bytes 4718596
